TPU v7x, 32 devices: a whole 2x2x4 slice. The times are simulated.
32 devices in a mesh: segment: 2 (over y), fsdp: 4 (over x, core), seq: 4 (over z).
Axes of the slice: x: 2, y: 2, z: 4, core: 2. Of those that a mesh axis runs over, the one named last changes fastest.
Arguments:
- arriving: bfloat16 [2, 4, 768, 2048], P('segment', 'fsdp', 'seq'), may hold values from -6 to 6
- gain: float32 [2, 2048], P('segment'), may hold values from 0.1 to 1.9
- input_weight: bfloat16 [2, 2048, 16, 3, 128], P('segment', 'fsdp', 'seq')
- output_weight: bfloat16 [2, 16, 128, 2048], P('segment', 'seq', None, 'fsdp'), may hold values from -1 to 1
- block_pattern: int32 [2, 4, 24, 6], P('segment', 'fsdp'), may hold values from 0 to 23, as said below
Outputs:
- passed: bfloat16 [2, 4, 768, 2048], P('segment', 'fsdp', 'seq')
Inputs may be any that keep to these rules, and one draw needn't show every extreme that they name: `block_pattern`: row j of a document lists 6 different blocks; the first three are j - 1, j and j + 1 modulo 24, and block 0 is listed in every row.
All inputs are finite; a program needn't handle non-finite values.
Results may differ from a plain program's by a relative error of at most 0.012.
Values may be sent and summed in bfloat16 or wider, within the bound.
A program may use at most 64 MiB of HBM per device.

v0:
```python
import jax
import jax.numpy as jnp
from jax import lax
from jax.sharding import PartitionSpec as P

BLOCK = 32
SEL = 6
EPSILON = 1e-05


def passed_along(value, axis, steps):
    count = lax.axis_size(axis)
    pairs = [(source, (source + steps) % count) for source in range(count)]
    return lax.ppermute(value, axis, pairs)


def normalize(tokens, gain_row):
    values = tokens.astype(jnp.float32)
    spread = jnp.mean(values * values, axis=-1, keepdims=True)
    return (values * lax.rsqrt(spread + EPSILON) * gain_row).astype(jnp.bfloat16)


def attend(projected, pattern_rows):
    length, head_group, triple, head_width = projected.shape
    block_count = length // BLOCK
    query_rows = projected[:, :, 0].reshape(block_count, BLOCK, head_group, head_width)
    key_blocks = projected[:, :, 1].reshape(block_count, BLOCK, head_group, head_width)
    value_blocks = projected[:, :, 2].reshape(block_count, BLOCK, head_group, head_width)
    key_rows = jnp.take(key_blocks, pattern_rows, axis=0).reshape(
        block_count, SEL * BLOCK, head_group, head_width
    )
    value_rows = jnp.take(value_blocks, pattern_rows, axis=0).reshape(
        block_count, SEL * BLOCK, head_group, head_width
    )
    scores = jnp.einsum(
        "qbge,qnge->gqbn", query_rows, key_rows, preferred_element_type=jnp.float32
    ) * head_width ** (-0.5)
    row_max = jnp.max(scores, axis=-1, keepdims=True)
    exponent = jnp.exp(scores - row_max)
    weights = (exponent / jnp.sum(exponent, axis=-1, keepdims=True)).astype(jnp.bfloat16)
    mixed_rows = jnp.einsum(
        "gqbn,qnge->qbge", weights, value_rows, preferred_element_type=jnp.float32
    )
    return mixed_rows.astype(jnp.bfloat16).reshape(length, head_group * head_width)


def body(arriving, gain, input_weight, output_weight, block_pattern):
    tokens = arriving[0, 0]
    row_count = tokens.shape[0]
    normed = normalize(tokens, gain[0])
    slab_rows, head_group, triple, head_size = input_weight.shape[1:]
    columns = head_group * triple * head_size
    panel_flat = input_weight[0].reshape(slab_rows, columns)
    length = row_count * lax.axis_size("seq")
    whole_panel = lax.all_gather(panel_flat, "fsdp", axis=0, tiled=True)
    projected = jnp.dot(
        lax.all_gather(normed, "seq", axis=0, tiled=True),
        whole_panel,
        preferred_element_type=jnp.float32,
    )
    projected = projected.astype(jnp.bfloat16).reshape(length, head_group, triple, head_size)
    mixed_rows = attend(projected, block_pattern[0, 0])
    out_panel = output_weight[0].reshape(head_group * head_size, -1)
    whole_out = lax.all_gather(out_panel, "fsdp", axis=1, tiled=True)
    branch = lax.psum_scatter(
        jnp.dot(mixed_rows, whole_out, preferred_element_type=jnp.float32).astype(jnp.bfloat16),
        "seq",
        scatter_dimension=0,
        tiled=True,
    ).astype(jnp.float32)
    updated = (tokens.astype(jnp.float32) + branch).astype(jnp.bfloat16)
    passed = passed_along(updated, "segment", 1)
    return passed[None, None]


def solution(mesh):
    in_specs = (
        P("segment", "fsdp", "seq", None),
        P("segment", None),
        P("segment", "fsdp", "seq", None, None),
        P("segment", "seq", None, "fsdp"),
        P("segment", "fsdp", None, None),
    )
    out_specs = P("segment", "fsdp", "seq", None)
    return jax.shard_map(body, mesh=mesh, in_specs=in_specs, out_specs=out_specs, check_vma=False)
```

profile of v0, /device:TPU:0, one launch (start us, length us, event | category | flops | bytes accessed | tf_op | source)
XLA Modules:
  0.0 277.0 jit_solution(2608817675597869169)
XLA Ops:
  6.5 1.5 fusion.4
  8.0 2.3 fusion.6
  10.4 2.6 copy.24
  13.0 0.7 all-gather.8.cloned.1.call-update
  14.1 62.6 %all-gather.4.cloned.1.call-done = bf16[768,2048]{1,0:T(8,128)(2,1)} async-done(((bf16[192,2048]{1,0:T(8,128)(2,1)}), bf16[768,2048]{1,0:T(8,128)(2,1)}) %all-gather.4.cloned.1.call-update) | async-done | bytes 3145744 | tf_op jit(solution)/shard_map/all_gather | solution.py:57
  76.7 46.6 %all-gather.6.cloned.1.call-done = bf16[2048,1536]{0,1:T(8,128)(2,1)} async-done(((bf16[512,1536]{0,1:T(8,128)(2,1)}), bf16[2048,1536]{0,1:T(8,128)(2,1)}) %all-gather.6.cloned.1.call-update) | async-done | bytes 6291472 | tf_op jit(solution)/shard_map/all_gather | solution.py:55
  123.3 9.3 %convolution_convert_fusion.1 = bf16[768,1536]{1,0:T(8,128)(2,1)} fusion(bf16[768,2048]{1,0:T(8,128)(2,1)} %all-gather.4.cloned.1.call-done, bf16[2048,1536]{0,1:T(8,128)(2,1)} %all-gather.6.cloned.1.call-done), kind=kOutput, calls=%fused_computation.6 | convolution fusion | flops 4833017856 | bytes 11796480 | tf_op jit(solution)/shard_map/dot_general | solution.py:56
  132.6 2.9 %copy.25 = bf16[768,1536]{0,1:T(8,128)(2,1)S(1)} copy(bf16[768,1536]{1,0:T(8,128)(2,1)} %convolution_convert_fusion.1) | data formatting | bytes 4718592 | tf_op jit(solution)/shard_map/convert_element_type | solution.py:61
  135.5 1.3 fusion.20
  136.8 1.5 copy.31
  138.3 1.5 copy.26
  139.8 7.6 %gather_fusion.1 = bf16[144,32,4,128]{3,1,2,0:T(8,128)(2,1)} fusion(bf16[24,32,4,128]{3,1,0,2:T(8,128)(2,1)S(1)} %bitcast.37, s32[1024]{0:T(1024)S(1)} %pad_clamp_fusion), kind=kCustom, calls=%fused_computation.1.clone | custom fusion | bytes 9437760 | tf_op jit(solution)/shard_map/jit(_take)/gather | solution.py:29
  147.4 7.6 %gather_fusion = bf16[144,32,4,128]{3,1,2,0:T(8,128)(2,1)} fusion(bf16[24,32,4,128]{3,1,0,2:T(8,128)(2,1)S(1)} %bitcast.36, s32[1024]{0:T(1024)S(1)} %pad_clamp_fusion), kind=kCustom, calls=%fused_computation.clone | custom fusion | bytes 9437760 | tf_op jit(solution)/shard_map/jit(_take)/gather | solution.py:32
  155.0 5.7 %broadcast_select_fusion = (bf16[24,6,32,4,128]{4,2,3,1,0:T(8,128)(2,1)S(1)}, bf16[24,6,32,4,128]{4,2,3,1,0:T(8,128)(2,1)}) fusion(bf16[24,6,32,4,128]{4,2,3,1,0:T(8,128)(2,1)} %bitcast.38, pred[24,6]{1,0:T(8,128)(4,1)S(1)} %copy.23, bf16[24,6,32,4,128]{4,2,3,1,0:T(8,128)(2,1)} %bitcast.39), kind=kLoop, calls=%fused_computation.3 | loop fusion | flops 4718592 | bytes 18874512 | tf_op jit(solution)/shard_map/jit(_take)/select_n | solution.py:29
  160.7 3.6 %copy.33 = bf16[24,6,32,4,128]{4,2,1,0,3:T(8,128)(2,1)} copy(bf16[24,6,32,4,128]{4,2,3,1,0:T(8,128)(2,1)S(1)} %get-tuple-element.9) | data formatting | bytes 9437184 | tf_op jit(solution)/shard_map/jit(_take)/select_n | solution.py:29
  164.6 5.9 %copy.28 = bf16[24,6,32,4,128]{4,2,1,3,0:T(8,128)(2,1)} copy(bf16[24,6,32,4,128]{4,2,3,1,0:T(8,128)(2,1)} %get-tuple-element.10) | data formatting | bytes 9437184 | tf_op jit(solution)/shard_map/jit(_take)/select_n | solution.py:32
  170.5 7.2 %fusion.21 = (f32[4,24,32]{2,1,0:T(8,128)S(1)}, f32[4,24,32,192]{3,2,1,0:T(8,128)}) fusion(bf16[24,32,4,128]{3,1,0,2:T(8,128)(2,1)S(1)} %bitcast.44, bf16[24,192,4,128]{3,1,0,2:T(8,128)(2,1)} %bitcast.40), kind=kOutput, calls=%fused_computation.31 | convolution fusion | flops 152764608 | bytes 7876608 | tf_op jit(solution)/shard_map/sub | solution.py:39
  177.7 5.2 %fusion.14 = bf16[24,32,4,128]{3,1,2,0:T(8,128)(2,1)S(1)} fusion(bf16[24,192,4,128]{3,1,2,0:T(8,128)(2,1)} %bitcast.43, f32[4,24,32,192]{3,2,1,0:T(8,128)} %get-tuple-element.12, f32[4,24,32]{2,1,0:T(8,128)S(1)} %get-tuple-element.11), kind=kOutput, calls=%fused_computation.22 | convolution fusion | flops 152567808 | bytes 7876608 | tf_op jit(solution)/shard_map/gqbn,qnge->qbge/dot_general | solution.py:41
  183.3 5.0 %convolution_convert_fusion = bf16[768,2048]{1,0:T(8,128)(2,1)} fusion(bf16[512,2048]{1,0:T(8,128)(2,1)} %all-gather.8.cloned.1.call-done, bf16[96,8,4,128]{3,2,1,0:T(4,128)(2,1)S(1)} %bitcast.45), kind=kOutput, calls=%fused_computation.5 | convolution fusion | flops 1612185600 | bytes 6029312 | tf_op jit(solution)/shard_map/dot_general | solution.py:66
  188.4 60.6 %reduce-scatter.2.cloned.1.call-done = bf16[192,2048]{1,0:T(8,128)(2,1)} async-done(((bf16[768,2048]{1,0:T(8,128)(2,1)}), bf16[192,2048]{1,0:T(8,128)(2,1)}) %reduce-scatter.2.cloned.1.call-update) | async-done | bytes 786448 | tf_op jit(solution)/shard_map/reduce_scatter | solution.py:65
  248.9 1.4 fusion.7
  250.4 1.5 collective-permute-start
  251.9 17.7 %collective-permute-done = bf16[192,2048]{1,0:T(8,128)(2,1)S(1)} collective-permute-done((bf16[192,2048]{1,0:T(8,128)(2,1)S(1)}, bf16[192,2048]{1,0:T(8,128)(2,1)S(1)}, u32[]{:S(2)}, u32[]{:S(2)}) %collective-permute-start) | collective-permute-done | bytes 786464 | tf_op jit(solution)/shard_map/ppermute | solution.py:14
  269.5 0.9 copy.52
  (23 shorter events, 1.3 us)
Async XLA Ops:
  6.5 3.8 %copy-start.1 = (bf16[1,512,4,3,128]{4,2,3,1,0:T(4,128)(2,1)S(1)}, bf16[1,512,4,3,128]{4,2,3,1,0:T(4,128)(2,1)}, u32[]{:S(2)}) copy-start(bf16[1,512,4,3,128]{4,2,3,1,0:T(4,128)(2,1)} %param.9) | copy-start | bytes 4718596
  6.5 70.1 %all-gather.4.cloned.1.call-start = ((), (), s32[]{:S(2)}) async-start(), calls=%async_computation.1 | async-start | bytes 3932160 | tf_op jit(solution)/shard_map/all_gather | solution.py:57
  10.3 3.5 %copy-start.2 = (s32[1,1,24,6]{2,1,3,0:T(1,128)S(1)}, s32[1,1,24,6]{2,1,3,0:T(1,128)}, u32[]{:S(2)}) copy-start(s32[1,1,24,6]{2,1,3,0:T(1,128)} %param.11) | copy-start | bytes 1732
  10.3 113.0 %all-gather.6.cloned.1.call-start = ((), (), s32[]{:S(2)}) async-start(), calls=%async_computation.2 | async-start | bytes 7864320 | tf_op jit(solution)/shard_map/all_gather | solution.py:55
  13.0 170.3 %all-gather.8.cloned.1.call-start = ((), (), s32[]{:S(2)}) async-start(), calls=%async_computation.3 | async-start | bytes 2621440 | tf_op jit(solution)/shard_map/all_gather | solution.py:64
  13.7 235.2 %reduce-scatter.2.cloned.1.call-start = ((), (), s32[]{:S(2)}) async-start(), calls=%async_computation.4 | async-start | bytes 3932160 | tf_op jit(solution)/shard_map/reduce_scatter | solution.py:65
  188.3 60.6 %copy-start = (bf16[1,1,192,2048]{3,2,1,0:T(8,128)(2,1)S(1)}, bf16[1,1,192,2048]{3,2,1,0:T(8,128)(2,1)}, u32[]{:S(2)}) copy-start(bf16[1,1,192,2048]{3,2,1,0:T(8,128)(2,1)} %param.7) | copy-start | bytes 2359300
  250.4 19.2 %collective-permute-start = (bf16[192,2048]{1,0:T(8,128)(2,1)S(1)}, bf16[192,2048]{1,0:T(8,128)(2,1)S(1)}, u32[]{:S(2)}, u32[]{:S(2)}) collective-permute-start(bf16[192,2048]{1,0:T(8,128)(2,1)S(1)} %fusion.7), channel_id=1, source_target_pairs={{0,16},{16,0},{1,17},{17,1},{2,18},{18,2},{3,19},{19,3},{4,20},{20... | collective-permute-start | bytes 2359304 | tf_op jit(solution)/shard_map/ppermute | solution.py:14
Sparse Core Ops, SparseCore 0:
  10.5 66.1 all-gather.3
  78.2 45.0 all-gather.5
  124.9 22.5 all-gather.7
  188.5 60.4 reduce-scatter.1
where the time goes:
time: 277 us
  waiting for transfers between devices  188 us (68%)
  local copies, waits for them, and re-layouts  36.4 us (13%)
  matrix products  26.7 us (10%)
  between operations  13.2 us (5%)
  other arithmetic  10.8 us (4%)
    all_gather x1, waiting for transfers between devices, body(): lax.all_gather(normed, 'seq', axis=0, tiled=True)  62.6 us
    reduce_scatter x1, waiting for transfers between devices, body(): lax.psum_scatter(jnp.dot(mixed_rows, whole_out, preferred_element_type=jn...  60.6 us
    all_gather x1, waiting for transfers between devices, body(): whole_panel = lax.all_gather(panel_flat, 'fsdp', axis=0, tiled=True)  46.6 us
    ppermute x1, waiting for transfers between devices, passed_along(): return lax.ppermute(value, axis, pairs)  17.7 us
    dot_general x1, matrix products, body(): jnp.dot(lax.all_gather(normed, 'seq', axis=0, tiled=True), whole_panel, p...  9.27 us
    gather x1, local copies, waits for them, and re-layouts, attend(): jnp.take(value_blocks, pattern_rows, axis=0)  7.62 us
    gather x1, local copies, waits for them, and re-layouts, attend(): jnp.take(key_blocks, pattern_rows, axis=0)  7.56 us
    sub x1, matrix products, attend(): exponent = jnp.exp(scores - row_max)  7.16 us
  transfers between devices with their start and end apart: 5, of which 4 were waited for; matrix products, arithmetic and copies ran while one was open for 23% of the time, Pallas kernels for 0%

commit v1 on v0

--- a/solution.py
+++ b/solution.py
@@ -6,6 +6,18 @@
 BLOCK = 32
 SEL = 6
 EPSILON = 1e-05
+
+
+def doubled_up(x, axis, dim):
+    ways, here = (lax.axis_size(axis), lax.axis_index(axis))
+    grown, reach = (x, 1)
+    while reach < ways:
+        theirs = lax.ppermute(grown, axis, [(d, d ^ reach) for d in range(ways)])
+        mine_first = jnp.concatenate([grown, theirs], axis=dim)
+        theirs_first = jnp.concatenate([theirs, grown], axis=dim)
+        grown = jnp.where(here & reach == 0, mine_first, theirs_first)
+        reach = 2 * reach
+    return grown
 
 
 def passed_along(value, axis, steps):
@@ -52,7 +64,7 @@
     columns = head_group * triple * head_size
     panel_flat = input_weight[0].reshape(slab_rows, columns)
     length = row_count * lax.axis_size("seq")
-    whole_panel = lax.all_gather(panel_flat, "fsdp", axis=0, tiled=True)
+    whole_panel = doubled_up(panel_flat, "fsdp", 0)
     projected = jnp.dot(
         lax.all_gather(normed, "seq", axis=0, tiled=True),
         whole_panel,

time: 277 us -> 251 us (0.906)
  waiting for transfers between devices: 188 us -> 155 us
  starting transfers between devices: 1.66 us -> 5 us
    ppermute x0 -> x2, waiting for transfers between devices: none -> 75 us  [doubled_up(): theirs = lax.ppermute(grown, axis, [(d, d ^ reach) for d in range(ways)])]
    all_gather x1, waiting for transfers between devices: 62.6 us -> 0.01 us  [body(): lax.all_gather(normed, 'seq', axis=0, tiled=True)]
    all_gather x1 -> x0, waiting for transfers between devices: 46.6 us -> none  [body(): whole_panel = lax.all_gather(panel_flat, 'fsdp', axis=0, tiled=True)]
    ppermute x0 -> x2, starting transfers between devices: none -> 3.38 us  [doubled_up(): theirs = lax.ppermute(grown, axis, [(d, d ^ reach) for d in range(ways)])]
  transfers between devices with their start and end apart: 5 -> 6, of which waited for: 4 -> 4; matrix products, arithmetic and copies ran while one was open for 23% -> 26% of each run, Pallas kernels for 0% -> 0%
where the time goes in v1:
time: 251 us; the launch traced here: 250 us
  waiting for transfers between devices  155 us (62%)
  local copies, waits for them, and re-layouts  35.2 us (14%)
  matrix products  28.6 us (11%)
  between operations  13.2 us (5%)
  other arithmetic  13 us (5%)
  starting transfers between devices  5 us (2%)
    ppermute x2, waiting for transfers between devices, doubled_up(): theirs = lax.ppermute(grown, axis, [(d, d ^ reach) for d in range(ways)])  75 us
    reduce_scatter x1, waiting for transfers between devices, body(): lax.psum_scatter(jnp.dot(mixed_rows, whole_out, preferred_element_type=jn...  62.7 us
    ppermute x1, waiting for transfers between devices, passed_along(): return lax.ppermute(value, axis, pairs)  17.6 us
    dot_general x1, matrix products, body(): jnp.dot(lax.all_gather(normed, 'seq', axis=0, tiled=True), whole_panel, p...  11.2 us
    gather x1, local copies, waits for them, and re-layouts, attend(): jnp.take(value_blocks, pattern_rows, axis=0)  7.62 us
    gather x1, local copies, waits for them, and re-layouts, attend(): jnp.take(key_blocks, pattern_rows, axis=0)  7.56 us
    sub x1, matrix products, attend(): exponent = jnp.exp(scores - row_max)  7.17 us
    select_n x2, local copies, waits for them, and re-layouts, attend(): jnp.take(value_blocks, pattern_rows, axis=0)  5.99 us
  transfers between devices with their start and end apart: 6, of which 4 were waited for; matrix products, arithmetic and copies ran while one was open for 26% of the time, Pallas kernels for 0%

profile of v1, /device:TPU:0, one launch (start us, length us, event | category | flops | bytes accessed | tf_op | source)
XLA Modules:
  0.0 250.4 jit_solution(10605426553385765655)
XLA Ops:
  6.5 1.5 fusion.12
  8.0 2.3 fusion.14
  10.4 1.4 copy.24
  12.3 3.0 %collective-permute-done = bf16[512,1536]{0,1:T(8,128)(2,1)S(1)} collective-permute-done((bf16[512,1536]{0,1:T(8,128)(2,1)S(1)}, bf16[512,1536]{0,1:T(8,128)(2,1)S(1)}, u32[]{:S(2)}, u32[]{:S(2)}) %collective-permute-start) | collective-permute-done | bytes 1572896 | tf_op jit(solution)/shard_map/ppermute | solution.py:15
  15.4 2.2 maximum_select_fusion.4
  17.5 2.9 %collective-permute-start.1 = (bf16[1024,1536]{0,1:T(8,128)(2,1)}, bf16[1024,1536]{0,1:T(8,128)(2,1)}, u32[]{:S(2)}, u32[]{:S(2)}) collective-permute-start(bf16[1024,1536]{0,1:T(8,128)(2,1)} %maximum_select_fusion.4), channel_id=1, source_target_pairs={{0,8},{4,12},{8,0},{12,4},{1,9},{5,13},{9,1},{13,5},{2,10},{6,14},... | collective-permute-start | bytes 9437192 | tf_op jit(solution)/shard_map/ppermute | solution.py:15
  20.8 71.9 %collective-permute-done.1 = bf16[1024,1536]{0,1:T(8,128)(2,1)} collective-permute-done((bf16[1024,1536]{0,1:T(8,128)(2,1)}, bf16[1024,1536]{0,1:T(8,128)(2,1)}, u32[]{:S(2)}, u32[]{:S(2)}) %collective-permute-start.1) | collective-permute-done | bytes 3145760 | tf_op jit(solution)/shard_map/ppermute | solution.py:15
  92.7 11.2 %fusion.8 = bf16[768,1536]{1,0:T(8,128)(2,1)} fusion(bf16[768,2048]{1,0:T(8,128)(2,1)} %all-gather.3.cloned.1.call-done, bf16[1024,1536]{0,1:T(8,128)(2,1)} %collective-permute-done.1, bf16[1024,1536]{0,1:T(8,128)(2,1)} %maximum_select_fusion.4, pred[]{:T(512)S(6)} %eq.6), kind=kOutput, calls=%fused_computation.13 | convolution fusion | flops 4861329408 | bytes 11796481 | tf_op jit(solution)/shard_map/dot_general | solution.py:68
  103.9 2.8 %copy.25 = bf16[768,1536]{0,1:T(8,128)(2,1)S(1)} copy(bf16[768,1536]{1,0:T(8,128)(2,1)} %fusion.8) | data formatting | bytes 4718592 | tf_op jit(solution)/shard_map/convert_element_type | solution.py:73
  106.8 1.3 fusion.29
  108.1 1.5 copy.31
  109.6 1.5 copy.26
  111.1 7.6 %gather_fusion.1 = bf16[144,32,4,128]{3,1,2,0:T(8,128)(2,1)} fusion(bf16[24,32,4,128]{3,1,0,2:T(8,128)(2,1)S(1)} %bitcast.36, s32[1024]{0:T(1024)S(1)} %pad_clamp_fusion), kind=kCustom, calls=%fused_computation.1.clone | custom fusion | bytes 9437760 | tf_op jit(solution)/shard_map/jit(_take)/gather | solution.py:41
  118.7 7.6 %gather_fusion = bf16[144,32,4,128]{3,1,2,0:T(8,128)(2,1)} fusion(bf16[24,32,4,128]{3,1,0,2:T(8,128)(2,1)S(1)} %bitcast.35, s32[1024]{0:T(1024)S(1)} %pad_clamp_fusion), kind=kCustom, calls=%fused_computation.clone | custom fusion | bytes 9437760 | tf_op jit(solution)/shard_map/jit(_take)/gather | solution.py:44
  126.3 5.7 %broadcast_select_fusion = (bf16[24,6,32,4,128]{4,2,3,1,0:T(8,128)(2,1)S(1)}, bf16[24,6,32,4,128]{4,2,3,1,0:T(8,128)(2,1)}) fusion(bf16[24,6,32,4,128]{4,2,3,1,0:T(8,128)(2,1)} %bitcast.37, pred[24,6]{1,0:T(8,128)(4,1)S(1)} %copy.23, bf16[24,6,32,4,128]{4,2,3,1,0:T(8,128)(2,1)} %bitcast.38), kind=kLoop, calls=%fused_computation.11 | loop fusion | flops 4718592 | bytes 18874512 | tf_op jit(solution)/shard_map/jit(_take)/select_n | solution.py:41
  131.9 3.6 %copy.33 = bf16[24,6,32,4,128]{4,2,1,0,3:T(8,128)(2,1)} copy(bf16[24,6,32,4,128]{4,2,3,1,0:T(8,128)(2,1)S(1)} %get-tuple-element.9) | data formatting | bytes 9437184 | tf_op jit(solution)/shard_map/jit(_take)/select_n | solution.py:41
  135.9 5.9 %copy.28 = bf16[24,6,32,4,128]{4,2,1,3,0:T(8,128)(2,1)} copy(bf16[24,6,32,4,128]{4,2,3,1,0:T(8,128)(2,1)} %get-tuple-element.10) | data formatting | bytes 9437184 | tf_op jit(solution)/shard_map/jit(_take)/select_n | solution.py:44
  141.8 7.2 %fusion.30 = (f32[4,24,32]{2,1,0:T(8,128)S(1)}, f32[4,24,32,192]{3,2,1,0:T(8,128)}) fusion(bf16[24,32,4,128]{3,1,0,2:T(8,128)(2,1)S(1)} %bitcast.44, bf16[24,192,4,128]{3,1,0,2:T(8,128)(2,1)} %bitcast.39), kind=kOutput, calls=%fused_computation.41 | convolution fusion | flops 152764608 | bytes 7876608 | tf_op jit(solution)/shard_map/sub | solution.py:51
  149.0 5.2 %fusion.22 = bf16[24,32,4,128]{3,1,2,0:T(8,128)(2,1)S(1)} fusion(bf16[24,192,4,128]{3,1,2,0:T(8,128)(2,1)} %bitcast.43, f32[4,24,32,192]{3,2,1,0:T(8,128)} %get-tuple-element.12, f32[4,24,32]{2,1,0:T(8,128)S(1)} %get-tuple-element.11), kind=kOutput, calls=%fused_computation.31 | convolution fusion | flops 152567808 | bytes 7876608 | tf_op jit(solution)/shard_map/gqbn,qnge->qbge/dot_general | solution.py:53
  154.6 5.0 %convolution_convert_fusion = bf16[768,2048]{1,0:T(8,128)(2,1)} fusion(bf16[512,2048]{1,0:T(8,128)(2,1)} %all-gather.5.cloned.1.call-done, bf16[96,8,4,128]{3,2,1,0:T(4,128)(2,1)S(1)} %bitcast.45), kind=kOutput, calls=%fused_computation.14 | convolution fusion | flops 1612185600 | bytes 6029312 | tf_op jit(solution)/shard_map/dot_general | solution.py:78
  159.7 62.7 %reduce-scatter.2.cloned.1.call-done = bf16[192,2048]{1,0:T(8,128)(2,1)} async-done(((bf16[768,2048]{1,0:T(8,128)(2,1)}), bf16[192,2048]{1,0:T(8,128)(2,1)}) %reduce-scatter.2.cloned.1.call-update) | async-done | bytes 786448 | tf_op jit(solution)/shard_map/reduce_scatter | solution.py:77
  222.4 1.4 fusion.15
  223.8 1.5 collective-permute-start.2
  225.3 17.6 %collective-permute-done.2 = bf16[192,2048]{1,0:T(8,128)(2,1)S(1)} collective-permute-done((bf16[192,2048]{1,0:T(8,128)(2,1)S(1)}, bf16[192,2048]{1,0:T(8,128)(2,1)S(1)}, u32[]{:S(2)}, u32[]{:S(2)}) %collective-permute-start.2) | collective-permute-done | bytes 786464 | tf_op jit(solution)/shard_map/ppermute | solution.py:26
  (25 shorter events, 2.7 us)
Async XLA Ops:
  6.5 3.8 %copy-start.1 = (bf16[1,512,4,3,128]{4,2,3,1,0:T(4,128)(2,1)S(1)}, bf16[1,512,4,3,128]{4,2,3,1,0:T(4,128)(2,1)}, u32[]{:S(2)}) copy-start(bf16[1,512,4,3,128]{4,2,3,1,0:T(4,128)(2,1)} %param.9) | copy-start | bytes 4718596
  6.5 86.2 %all-gather.3.cloned.1.call-start = ((), (), s32[]{:S(2)}) async-start(), calls=%async_computation.1 | async-start | bytes 3932160 | tf_op jit(solution)/shard_map/all_gather | solution.py:69
  10.3 144.3 %all-gather.5.cloned.1.call-start = ((), (), s32[]{:S(2)}) async-start(), calls=%async_computation.2 | async-start | bytes 2621440 | tf_op jit(solution)/shard_map/all_gather | solution.py:76
  11.8 3.6 %collective-permute-start = (bf16[512,1536]{0,1:T(8,128)(2,1)S(1)}, bf16[512,1536]{0,1:T(8,128)(2,1)S(1)}, u32[]{:S(2)}, u32[]{:S(2)}) collective-permute-start(bf16[512,1536]{0,1:T(8,128)(2,1)S(1)} %bitcast.41), channel_id=1, source_target_pairs={{0,4},{4,0},{8,12},{12,8},{1,5},{5,1},{9,13},{13,9},{2,6},{6,2},{1... | collective-permute-start | bytes 4718600 | tf_op jit(solution)/shard_map/ppermute | solution.py:15
  12.3 8.1 %copy-start.2 = (s32[1,1,24,6]{2,1,3,0:T(1,128)S(1)}, s32[1,1,24,6]{2,1,3,0:T(1,128)}, u32[]{:S(2)}) copy-start(s32[1,1,24,6]{2,1,3,0:T(1,128)} %param.11) | copy-start | bytes 1732
  17.5 75.2 %collective-permute-start.1 = (bf16[1024,1536]{0,1:T(8,128)(2,1)}, bf16[1024,1536]{0,1:T(8,128)(2,1)}, u32[]{:S(2)}, u32[]{:S(2)}) collective-permute-start(bf16[1024,1536]{0,1:T(8,128)(2,1)} %maximum_select_fusion.4), channel_id=1, source_target_pairs={{0,8},{4,12},{8,0},{12,4},{1,9},{5,13},{9,1},{13,5},{2,10},{6,14},... | collective-permute-start | bytes 9437192 | tf_op jit(solution)/shard_map/ppermute | solution.py:15
  20.4 202.0 %reduce-scatter.2.cloned.1.call-start = ((), (), s32[]{:S(2)}) async-start(), calls=%async_computation.3 | async-start | bytes 3932160 | tf_op jit(solution)/shard_map/reduce_scatter | solution.py:77
  159.6 62.8 %copy-start = (bf16[1,1,192,2048]{3,2,1,0:T(8,128)(2,1)S(1)}, bf16[1,1,192,2048]{3,2,1,0:T(8,128)(2,1)}, u32[]{:S(2)}) copy-start(bf16[1,1,192,2048]{3,2,1,0:T(8,128)(2,1)} %param.7) | copy-start | bytes 2359300
  223.8 19.2 %collective-permute-start.2 = (bf16[192,2048]{1,0:T(8,128)(2,1)S(1)}, bf16[192,2048]{1,0:T(8,128)(2,1)S(1)}, u32[]{:S(2)}, u32[]{:S(2)}) collective-permute-start(bf16[192,2048]{1,0:T(8,128)(2,1)S(1)} %fusion.15), channel_id=1, source_target_pairs={{0,16},{16,0},{1,17},{17,1},{2,18},{18,2},{3,19},{19,3},{4,20},{20... | collective-permute-start | bytes 2359304 | tf_op jit(solution)/shard_map/ppermute | solution.py:26
Sparse Core Ops, SparseCore 0:
  10.4 66.1 all-gather.2
  78.2 23.4 all-gather.4
  159.8 62.5 reduce-scatter.1
